TPU v7x, 128 devices: a whole 4x4x4 slice. The times are simulated.
128 devices in a mesh: blk: 32 (over y, z_lo, x), rep: 4 (over z_hi, core).
Axes of the slice: x: 4, y: 4, z: 4 (z_hi: 2, z_lo: 2; z = z_hi * 2 + z_lo), core: 2. Of those that a mesh axis runs over, the one named last changes fastest.
Arguments:
- loads: bfloat16 [24576, 512], P('blk', 'rep'), may hold values from -6 to 6
- values: bfloat16 [9216, 192, 192], P('blk'), may hold values from -0.0390625 to 0.0390625
- row_ptr: int32 [32, 5], P('blk'), may hold values from 0 to 288, as said below
- col_idx: int32 [9216], P('blk'), may hold values from 0 to 127
- elem_vals: bfloat16 [4096, 192, 192], P(('blk', 'rep')), may hold values from -0.0390625 to 0.0390625
- elem_owner: int32 [4096, 1], P(('blk', 'rep')), may hold values from 0 to 31; in each aligned block of 32 rows (0 to 31, 32 to 63, ...) at most 2 rows name the same one
- elem_row: int32 [4096], P(('blk', 'rep')), may hold values from 0 to 3
- elem_col: int32 [4096], P(('blk', 'rep')), may hold values from 0 to 127
Outputs:
- response: float32 [24576, 512], P('blk', 'rep')
Inputs may be any that keep to these rules, and one draw needn't show every extreme that they name: Pointers don't fall along a row; each block row holds 36 to 72 slots; row_ptr[b, 0] = 0, and on some index of blk the last pointer is 288. `elem_owner`: among the 32 elements of one device, no owner is named more than 2 times, a bound that some block reaches.
All inputs are finite; a program needn't handle non-finite values.
Results may differ from a plain program's by a relative error of at most 0.0029.
Values may be sent and summed in bfloat16 or wider, within the bound.
A program may use at most 192 MiB of HBM per device.

v0:
```python
import functools

import jax
import jax.numpy as jnp
from jax import lax
from jax.experimental import pallas as pl
from jax.experimental.pallas import tpu as pltpu
from jax.sharding import PartitionSpec as P

MESH = pl.DeviceIdType.MESH
BS = 192
ROWS = 768
LANES = 128
HALF = ROWS // 2
PAIR = 3 * BS
CHUNK = 16
DEPTH = 4


class Place:
    def __init__(self):
        blk = lax.axis_index("blk")
        rep = lax.axis_index("rep")
        self.x = lax.rem(blk, 4)
        self.zl = lax.rem(blk // 4, 2)
        self.y = blk // 8
        self.zh = rep // 2
        self.core = lax.rem(rep, 2)

    def block(self, dx, dy, dz):
        x = lax.rem(self.x + dx, 4)
        y = lax.rem(self.y + dy, 4)
        zl = lax.rem(self.zl + dz, 2)
        return (y * 2 + zl) * 4 + x

    def above(self, dz):
        z = lax.rem(self.zh * 2 + self.zl + dz, 4)
        return ((self.y * 2 + lax.rem(z, 2)) * 4 + self.x, (z // 2) * 2 + self.core)

    def device(self, dx, dy, dz, dzh=0, dcore=0):
        zh = lax.rem(self.zh + dzh, 2)
        core = lax.rem(self.core + dcore, 2)
        return (self.block(dx, dy, dz), zh * 2 + core)


SHIFTS = (
    (0, 0), (2, 2), (1, 1), (3, 3), (1, 3), (3, 1), (2, 1), (2, 3),
    (1, 2), (3, 2), (1, 0), (3, 0), (0, 1), (0, 3), (2, 0), (0, 2),
)


def shift(q):
    dx = dy = 0
    for i, (a, b) in enumerate(SHIFTS):
        dx = jnp.where(q == i, a, dx)
        dy = jnp.where(q == i, b, dy)
    return dx, dy


def wait_bytes(ref, sem):
    pltpu.make_async_copy(ref, ref, sem).wait()


class Gather:
    def __init__(self, place, g, late, sems):
        self.place = place
        self.g = g
        self.late = late
        (self.sends, self.cross_s, self.cross_r, self.sem_z, self.sem1, self.sem1f, self.sem2, self.sem2f, self.sem_l) = sems
        self.lanes = pl.ds(pl.multiple_of(place.core * LANES, LANES), LANES)
        self.other = pl.ds(pl.multiple_of((1 - place.core) * LANES, LANES), LANES)

    def peers(self):
        p = self.place
        return [
            p.device(0, 0, 1),
            p.device(1, 0, 0),
            p.device(3, 0, 0),
            p.device(0, 1, 0),
            p.device(0, 3, 0),
            p.device(0, 0, 0, 0, 1),
        ]

    def rows(self, dz):
        return HALF if dz == 0 else HALF - self.late

    def piece(self, half, p1, p2, dz, start=0, size=None):
        block = self.place.block(p1, p2, dz) if half == 0 else self.place.block(p2, p1, dz)
        first = pl.multiple_of(block * ROWS + (half * HALF + start), 64)
        return self.g.at[pl.ds(first, self.rows(dz) if size is None else size), self.lanes]

    def part(self, half, p1, p2, dz, way):
        size = self.rows(dz) // 2
        return self.piece(half, p1, p2, dz, way * size, size)

    def peer(self, half, stage, step):
        along_x = (half == 0) == (stage == 1)
        return self.place.device(step, 0, 0) if along_x else self.place.device(0, step, 0)

    def send(self, ref, device, sem):
        pltpu.make_async_remote_copy(ref, ref, self.sends, sem, device_id=device, device_id_type=MESH).start()

    def cross(self, ref):
        pltpu.make_async_remote_copy(
            ref, ref, self.cross_s, self.cross_r, device_id=self.place.device(0, 0, 0, 0, 1), device_id_type=MESH
        ).start()

    def chunk(self):
        first = pl.multiple_of(self.place.block(0, 0, 0) * ROWS, ROWS)
        return self.g.at[pl.ds(first, ROWS), self.lanes]

    def start(self):
        for half in (0, 1):
            self.send(
                self.piece(half, 0, 0, 0, 0, HALF - self.late), self.place.device(0, 0, 1), self.sem_z.at[half]
            )
        self.spread1(0)
        for half in (0, 1):
            self.spread2(half, 0, 0, 0)
            self.give_late(half, 0, 0)
        self.cross(self.chunk())

    def spread1(self, dz):
        for half in (0, 1):
            for way in (0, 1):
                self.send(
                    self.piece(half, 0, 0, dz), self.peer(half, 1, 1 if way == 0 else 3), self.sem1.at[half, dz, way]
                )

    def spread2(self, half, q, p1, dz):
        for way in (0, 1):
            self.send(
                self.piece(half, p1, 0, dz), self.peer(half, 2, 1 if way == 0 else 3), self.sem2.at[half, q, dz, way]
            )

    def give_late(self, half, p1, p2):
        if self.late:
            self.send(
                self.piece(half, p1, p2, 0, HALF - self.late, self.late),
                self.place.device(0, 0, 1),
                self.sem_l.at[half, p1, p2],
            )

    def take_late(self, p1, p2):
        if self.late:
            for half in (0, 1):
                got = self.piece(half, p1, p2, 1, HALF - self.late, self.late)
                wait_bytes(got, self.sem_l.at[half, p1, p2])
                self.cross(got)

    def neighbour_z(self):
        for half in (0, 1):
            wait_bytes(self.piece(half, 0, 0, 1), self.sem_z.at[half])
        self.spread1(1)
        for half in (0, 1):
            self.spread2(half, 0, 0, 1)
            self.cross(self.piece(half, 0, 0, 1))

    def pass1(self, dz):
        for half in (0, 1):
            for way in (0, 1):
                p1 = 3 if way == 0 else 1
                got = self.piece(half, p1, 0, dz)
                wait_bytes(got, self.sem1.at[half, dz, way])
                self.send(
                    self.part(half, p1, 0, dz, way),
                    self.peer(half, 1, 1 if way == 0 else 3),
                    self.sem1f.at[half, dz, way],
                )
                self.spread2(half, 2 if p1 == 3 else 1, p1, dz)
                self.cross(got)
                if dz == 0:
                    self.give_late(half, p1, 0)

    def far1(self, dz):
        for half in (0, 1):
            for way in (0, 1):
                wait_bytes(self.part(half, 2, 0, dz, way), self.sem1f.at[half, dz, way])
            self.spread2(half, 3, 2, dz)
            self.cross(self.piece(half, 2, 0, dz))
            if dz == 0:
                self.give_late(half, 2, 0)

    def pass2(self, q, dz):
        p1 = q ^ (q // 2)
        for half in (0, 1):
            for way in (0, 1):
                p2 = 3 if way == 0 else 1
                got = self.piece(half, p1, p2, dz)
                wait_bytes(got, self.sem2.at[half, q, dz, way])
                self.send(
                    self.part(half, p1, p2, dz, way),
                    self.peer(half, 2, 1 if way == 0 else 3),
                    self.sem2f.at[half, q, dz, way],
                )
                self.cross(got)
                if dz == 0:
                    self.give_late(half, p1, p2)

    def far2(self, q, dz):
        p1 = q ^ (q // 2)
        for half in (0, 1):
            for way in (0, 1):
                wait_bytes(self.part(half, p1, 2, dz, way), self.sem2f.at[half, q, dz, way])
            self.cross(self.piece(half, p1, 2, dz))
            if dz == 0:
                self.give_late(half, p1, 2)

    def finish(self):
        wait_bytes(self.g.at[:, self.other], self.cross_r)
        wait_bytes(self.g.at[:, self.lanes], self.cross_s)
        wait_bytes(self.g.at[pl.ds(0, 31 * ROWS), self.lanes], self.sends)


def gather_scratch():
    dma = pltpu.SemaphoreType.DMA
    return [
        dma,
        dma,
        dma,
        dma((2,)),
        dma((2, 2, 2)),
        dma((2, 2, 2)),
        dma((2, 4, 2, 2)),
        dma((2, 4, 2, 2)),
        dma((2, 4, 4)),
    ]


def greet(devices):
    barrier = pltpu.get_barrier_semaphore()
    for device in devices:
        pl.semaphore_signal(barrier, inc=1, device_id=device, device_id_type=MESH)
    return barrier


def exchange_kernel(loads, elems, places, codes, g, r, table, m, t, held, packed, ed, es, er, ee, eo, ms, mz, mr, mzr, own, hsem, *sems):
    place = Place()
    r = r.reshape(4, 16, PAIR, LANES)
    gather = Gather(place, g.reshape(32 * ROWS, 2 * LANES), 0, sems)
    spot = place.y * 4 + place.x
    level = place.zh * 2 + place.zl
    barrier = greet(gather.peers() + [place.above(dz) for dz in (1, 2, 3)])

    def greet_step(q, _):
        dx, dy = shift(q)
        pl.semaphore_signal(barrier, inc=1, device_id=place.device(dx, dy, 0), device_id_type=MESH)
        return 0

    lax.fori_loop(1, 16, greet_step, 0)
    mine = pltpu.make_async_copy(loads, gather.chunk(), own)
    mine.start()
    holding = pltpu.make_async_copy(elems, held, hsem)
    holding.start()

    mine.wait()
    pl.semaphore_wait(barrier, 6 + 3 + 15)

    def send(source, target, send_sem, recv_sem, device):
        pltpu.make_async_remote_copy(
            source, target, send_sem, recv_sem, device_id=device, device_id_type=MESH
        ).start()

    def pack(q, dx, dy):
        for dz in (0, 1):
            target = place.block(dx, dy, dz)
            one = held[places[target * 2]]
            two = held[places[target * 2 + 1]]
            packed[q, dz, pl.ds(0, BS), :] = one[:, :LANES]
            packed[q, dz, pl.ds(BS, BS), :] = two[:, :LANES]
            packed[q, dz, pl.ds(2 * BS, BS), :] = jnp.concatenate([one[:, LANES:], two[:, LANES:]], axis=1)

    def hand_on(mine, others, at):
        send(mine, r.at[level, at], es, er, place.above(2))
        send(others, r.at[level, at], es, er, place.above(1))
        send(others, r.at[level, at], es, er, place.above(3))

    def elements(q):
        dx, dy = shift(q)
        pack(q, dx, dy)
        device = place.device(dx, dy, 0)
        send(packed.at[q, 0], r.at[level, spot], ed, ee.at[q], device)
        send(packed.at[q, 1], t.at[spot], ed, eo.at[q], device)
        send(codes, m.at[level, spot], ms, mr, device)

    def own_elements():
        pack(0, 0, 0)
        hand_on(packed.at[0, 0], packed.at[0, 1], spot)
        pltpu.make_async_copy(packed.at[0, 0], r.at[level, spot], ee.at[0]).start()
        pltpu.make_async_copy(packed.at[0, 1], t.at[spot], eo.at[0]).start()
        pltpu.make_async_copy(codes, m.at[level, spot], mr).start()

    def relay(q):
        dx, dy = shift(q)
        at = lax.rem(place.y + 4 - dy, 4) * 4 + lax.rem(place.x + 4 - dx, 4)
        wait_bytes(r.at[level, at], ee.at[q])
        wait_bytes(t.at[at], eo.at[q])
        hand_on(r.at[level, at], t.at[at], at)

    def loop(first, last, step):
        def one(k, _):
            step(k)
            return 0

        lax.fori_loop(first, last, one, 0)

    holding.wait()
    own_elements()
    loop(1, 16, elements)
    gather.start()
    loop(1, 16, relay)
    gather.pass1(0)
    gather.neighbour_z()
    gather.far1(0)
    loop(0, 3, lambda q: gather.pass2(q, 0))
    gather.pass1(1)
    loop(3, 4, lambda q: gather.pass2(q, 0))
    gather.far1(1)
    loop(0, 4, lambda q: gather.far2(q, 0))
    loop(0, 4, lambda q: gather.pass2(q, 1))
    loop(0, 4, lambda q: gather.far2(q, 1))
    wait_bytes(r.at[level, spot], ee.at[0])
    wait_bytes(t.at[spot], eo.at[0])
    wait_bytes(m.at[level], mr)
    for dz in (1, 2, 3):
        send(m.at[level], m.at[level], mz, mzr, place.above(dz))
    gather.finish()
    wait_bytes(r.at[pl.ds(0, 3)], er)
    wait_bytes(m.at[pl.ds(0, 3)], mzr)
    wait_bytes(r.at[pl.ds(0, 3)], es)
    wait_bytes(packed.at[pl.ds(0, 15)], ed)
    wait_bytes(m.at[0, pl.ds(0, 15)], ms)
    wait_bytes(m.at[pl.ds(0, 3)], mz)
    table[...] = m[:, :, 0, :].reshape(64, LANES)


def exchange(loads, elems, places, codes):
    hbm = pl.BlockSpec(memory_space=pltpu.HBM)
    vmem = pl.BlockSpec(memory_space=pltpu.VMEM)
    dma = pltpu.SemaphoreType.DMA
    return pl.pallas_call(
        exchange_kernel,
        out_shape=[
            pltpu.VMEM((128, BS, 2 * LANES), jnp.bfloat16),
            pltpu.VMEM((64, PAIR, LANES), jnp.bfloat16),
            pltpu.VMEM((64, LANES), jnp.int32),
        ],
        in_specs=[
            hbm,
            hbm,
            pl.BlockSpec(memory_space=pltpu.SMEM),
            hbm,
        ],
        out_specs=[vmem, vmem, vmem],
        scratch_shapes=[
            pltpu.VMEM((4, 16, 8, LANES), jnp.int32),
            pltpu.VMEM((16, PAIR, LANES), jnp.bfloat16),
            pltpu.VMEM(elems.shape, jnp.bfloat16),
            pltpu.VMEM((16, 2, PAIR, LANES), jnp.bfloat16),
            dma,
            dma,
            dma,
            dma((16,)),
            dma((16,)),
            dma,
            dma,
            dma,
            dma,
            dma,
            dma,
            *gather_scratch(),
        ],
        compiler_params=pltpu.CompilerParams(collective_id=1, has_side_effects=True, vmem_limit_bytes=30 << 20),
        name="exchange",
    )(loads, elems, places, codes)


def share_sum(place, part, came, send_sem, recv_sem):
    lanes = pl.ds(pl.multiple_of(place.core * LANES, LANES), LANES)
    other = pl.ds(pl.multiple_of((1 - place.core) * LANES, LANES), LANES)
    copy = pltpu.make_async_remote_copy(
        part.at[:, other], came, send_sem, recv_sem, device_id=place.device(0, 0, 0, 0, 1), device_id_type=MESH
    )
    copy.start()
    copy.wait()
    return part[:, lanes] + came[...]


def gather_kernel(part, g, came, send_sem, recv_sem, *sems):
    place = Place()
    gather = Gather(place, g.reshape(32 * ROWS, 2 * LANES), 128, sems)
    barrier = greet(gather.peers())
    pl.semaphore_wait(barrier, 6)
    gather.chunk()[...] = share_sum(place, part, came, send_sem, recv_sem).astype(jnp.bfloat16)
    gather.start()
    gather.pass1(0)
    gather.neighbour_z()
    gather.far1(0)

    def loop(first, last, step):
        def one(q, _):
            step(q)
            return 0

        lax.fori_loop(first, last, one, 0)

    loop(0, 3, lambda q: gather.pass2(q, 0))
    gather.pass1(1)
    loop(3, 4, lambda q: gather.pass2(q, 0))
    gather.far1(1)
    loop(0, 4, lambda q: gather.far2(q, 0))

    def step2(q):
        gather.pass2(q, 1)
        gather.take_late(q, 0)

    loop(0, 4, step2)

    def step3(q):
        gather.far2(q, 1)
        gather.take_late(q, 1)
        gather.take_late(q, 3)

    loop(0, 4, step3)
    loop(0, 4, lambda q: gather.take_late(q, 2))
    gather.finish()


def gather_first(part):
    dma = pltpu.SemaphoreType.DMA
    return pl.pallas_call(
        gather_kernel,
        out_shape=pltpu.VMEM((128, BS, 2 * LANES), jnp.bfloat16),
        in_specs=[pl.BlockSpec(memory_space=pltpu.VMEM)],
        out_specs=pl.BlockSpec(memory_space=pltpu.VMEM),
        scratch_shapes=[
            pltpu.VMEM((ROWS, LANES), jnp.float32),
            dma,
            dma,
            *gather_scratch(),
        ],
        compiler_params=pltpu.CompilerParams(collective_id=2, has_side_effects=True, vmem_limit_bytes=4 << 20),
        name="gather_first",
    )(part)


def sum_kernel(part, out, came, send_sem, recv_sem):
    place = Place()
    barrier = greet([place.device(0, 0, 0, 0, 1)])
    pl.semaphore_wait(barrier, 1)
    out[...] = share_sum(place, part, came, send_sem, recv_sem)


def sum_cores(part):
    dma = pltpu.SemaphoreType.DMA
    return pl.pallas_call(
        sum_kernel,
        out_shape=jax.ShapeDtypeStruct((ROWS, LANES), jnp.float32),
        in_specs=[pl.BlockSpec(memory_space=pltpu.VMEM)],
        out_specs=pl.BlockSpec(memory_space=pltpu.VMEM),
        scratch_shapes=[pltpu.VMEM((ROWS, LANES), jnp.float32), dma, dma],
        compiler_params=pltpu.CompilerParams(collective_id=3, has_side_effects=True, vmem_limit_bytes=4 << 20),
        name="sum_cores",
    )(part)


def product_kernel(row_of, col_idx, table, vals, pairs, panel, out, vbuf, acc, code, sem, vsem):
    fetch = pltpu.make_async_copy(table, code, sem)
    fetch.start()
    core = lax.rem(lax.axis_index("rep"), 2)
    blk = lax.axis_index("blk")
    v_count = vals.shape[0] // (2 * CHUNK)

    def v_copy(j, slot):
        first = (2 * j + core) * CHUNK
        return pltpu.make_async_copy(vals.at[pl.ds(first, CHUNK)], vbuf.at[slot], vsem.at[slot])

    for j in range(DEPTH):
        v_copy(j, j).start()
    acc[...] = jnp.zeros_like(acc)
    none = jnp.zeros((64, 2 * LANES), jnp.bfloat16)
    fetch.wait()

    def e_step(j, _):
        for u in range(2 * CHUNK):
            at = j * CHUNK + u // 2
            held = code[at, blk * 2 + u % 2]
            row = lax.shift_right_logical(held, 7)
            x = panel[held & 127]
            ends = [x[LANES:], none] if u % 2 == 0 else [none, x[LANES:]]
            block = jnp.concatenate([pairs[at, pl.ds(u % 2 * BS, BS)], pairs[at, pl.ds(2 * BS, BS)]], axis=1)
            acc[row] += jnp.dot(
                block, jnp.concatenate([x[:LANES], *ends], axis=0), preferred_element_type=jnp.float32
            )
        return 0

    lax.fori_loop(0, pairs.shape[0] // CHUNK, e_step, 0)

    def v_step(j, _):
        slot = lax.rem(j, DEPTH)
        v_copy(j, slot).wait()
        for u in range(CHUNK):
            s = (2 * j + core) * CHUNK + u
            acc[row_of[s]] += jnp.dot(vbuf[slot, u], panel[col_idx[s]], preferred_element_type=jnp.float32)

        @pl.when(j + DEPTH < v_count)
        def _():
            v_copy(j + DEPTH, slot).start()

        return 0

    lax.fori_loop(0, v_count, v_step, 0)
    out[...] = acc[1:].reshape(out.shape)


def products(row_of, col_idx, table, vals, elems, g):
    smem = pl.BlockSpec(memory_space=pltpu.SMEM)
    vmem = pl.BlockSpec(memory_space=pltpu.VMEM)
    hbm = pl.BlockSpec(memory_space=pltpu.HBM)
    return pl.pallas_call(
        product_kernel,
        out_shape=pltpu.VMEM((ROWS, 2 * LANES), jnp.float32),
        in_specs=[smem, smem, vmem, hbm, vmem, vmem],
        out_specs=vmem,
        scratch_shapes=[
            pltpu.VMEM((DEPTH, CHUNK, BS, BS), jnp.bfloat16),
            pltpu.VMEM((5, BS, 2 * LANES), jnp.float32),
            pltpu.SMEM((64, LANES), jnp.int32),
            pltpu.SemaphoreType.DMA,
            pltpu.SemaphoreType.DMA((DEPTH,)),
        ],
        compiler_params=pltpu.CompilerParams(vmem_limit_bytes=12 << 20),
        name="products",
    )(row_of, col_idx, table, vals, elems, g)


def body(loads, values, row_ptr, col_idx, elem_vals, elem_owner, elem_row, elem_col):
    owners = elem_owner[:, 0]
    count = owners.shape[0]
    order = jnp.arange(count, dtype=jnp.int32)
    earlier = (owners[:, None] == owners[None, :]) & (order[None, :] < order[:, None])
    rank = jnp.sum(earlier.astype(jnp.int32), axis=1)
    slot = owners * 2 + rank
    taken = slot[None, :] == jnp.arange(LANES, dtype=jnp.int32)[:, None]
    places = jnp.sum(jnp.where(taken, order[None, :], 0), axis=1)
    code = jnp.sum(jnp.where(taken, ((elem_row + 1) * 128 + elem_col)[None, :], 0), axis=1)
    codes = jnp.broadcast_to(code[None, :], (8, LANES))
    positions = jnp.arange(values.shape[0], dtype=jnp.int32)
    row = 1 + jnp.sum((positions[:, None] >= row_ptr[0, 1:][None, :]).astype(jnp.int32), axis=1)
    row_of = jnp.where(row > 4, 0, row)
    g, r, table = exchange(loads, elem_vals, places, codes)

    apply = functools.partial(products, row_of, col_idx, table, values, r)
    part = apply(g)
    g2 = gather_first(part)
    return sum_cores(apply(g2))


def solution(mesh):
    placed = (
        P("blk", "rep"),
        P("blk", None, None),
        P("blk", None),
        P("blk"),
        P(("blk", "rep"), None, None),
        P(("blk", "rep"), None),
        P(("blk", "rep")),
        P(("blk", "rep")),
    )
    return jax.shard_map(body, mesh=mesh, in_specs=placed, out_specs=P("blk", "rep"), check_vma=False)
```

profile of v0, /device:TPU:0, one launch (start us, length us, event | category | flops | bytes accessed | tf_op | source)
XLA Modules:
  0.0 189.5 jit_solution(10712364665498286959)
XLA Ops:
  0.0 0.7 slice_bitcast_fusion
  0.7 0.9 convert_reduce_fusion
  1.6 0.7 multiply_add_fusion
  2.3 0.1 select_reduce_fusion
  2.4 0.1 convert_reduce_fusion.1
  2.5 0.0 copy-start
  2.5 0.9 copy-done
  3.5 120.5 %exchange.1 = (bf16[128,192,256]{2,1,0:T(8,128)(2,1)S(1)}, bf16[64,576,128]{2,1,0:T(8,128)(2,1)S(1)}, s32[64,128]{1,0:T(8,128)S(1)}) custom-call(bf16[768,128]{1,0:T(8,128)(2,1)S(1)} %copy-done, bf16[32,192,192]{2,1,0:T(8,128)(2,1)} %elems.1, s32[128]{0:T(128)S(1)} %get-tuple-element.12.places, s32[8,128]{1,0:T(8,128)S(1)} %broadcast_in_dim.39.codes), custom_call_target="tpu_custom_call" | custom-call | tf_op jit(solution)/shard_map/exchange/pallas_call | solution.py:341
  123.9 0.0 copy-start.1
  124.0 0.7 copy-done.1
  124.6 12.5 %products.2.part = f32[768,256]{1,0:T(8,128)S(1)} custom-call(s32[288]{0:T(512)S(1)} %compare_select_fusion.row_of, s32[288]{0:T(512)S(1)} %copy-done.1, s32[64,128]{1,0:T(8,128)S(1)} %get-tuple-element.8.table, bf16[288,192,192]{2,1,0:T(8,128)(2,1)} %vals.3, bf16[64,576,128]{2,1,0:T(8,128)(2,1)S(1)} %get-tuple-element.9.pairs, ...), custom_call_target="tpu_custom_call" | custom-call | tf_op jit(solution)/shard_map/products/pallas_call | solution.py:520
  137.1 37.3 %gather_first.1.panel = bf16[128,192,256]{2,1,0:T(8,128)(2,1)S(1)} custom-call(f32[768,256]{1,0:T(8,128)S(1)} %products.2.part), custom_call_target="tpu_custom_call" | custom-call | tf_op jit(solution)/shard_map/gather_first/pallas_call | solution.py:431
  174.4 12.5 %products.3.part = f32[768,256]{1,0:T(8,128)S(1)} custom-call(s32[288]{0:T(512)S(1)} %compare_select_fusion.row_of, s32[288]{0:T(512)S(1)} %copy-done.1, s32[64,128]{1,0:T(8,128)S(1)} %get-tuple-element.8.table, bf16[288,192,192]{2,1,0:T(8,128)(2,1)} %vals.3, bf16[64,576,128]{2,1,0:T(8,128)(2,1)S(1)} %get-tuple-element.9.pairs, ...), custom_call_target="tpu_custom_call" | custom-call | tf_op jit(solution)/shard_map/products/pallas_call | solution.py:520
  186.9 1.9 sum_cores.1
  188.8 0.7 copy.10
  (2 shorter events, 0.0 us)
Async XLA Ops:
  2.5 0.9 copy-start
  123.9 0.7 copy-start.1
where the time goes:
time: 191 us; the launch traced here: 190 us
  Pallas kernels  185 us (97%)
  local copies, waits for them, and re-layouts  3.08 us (2%)
    pallas_call x1, Pallas kernels, exchange(): pl.pallas_call(exchange_kernel, out_shape=[pltpu.VMEM((128, BS, 2 * LANES...  120 us
    pallas_call x1, Pallas kernels, gather_first(): pl.pallas_call(gather_kernel, out_shape=pltpu.VMEM((128, BS, 2 * LANES),...  37.3 us
    pallas_call x2, Pallas kernels, products(): pl.pallas_call(product_kernel, out_shape=pltpu.VMEM((ROWS, 2 * LANES), jn...  24.9 us

commit v1 on v0

--- a/solution.py
+++ b/solution.py
@@ -15,6 +15,7 @@
 PAIR = 3 * BS
 CHUNK = 16
 DEPTH = 4
+STORED_ROWS = ((0, 1, (0,)), (1, 2, (0, 1)), (2, 3, (0, 1, 2)), (3, 5, (1, 2, 3)), (5, 7, (2, 3)), (7, 9, (3,)))
 
 
 class Place:
@@ -234,7 +235,7 @@
     return barrier
 
 
-def exchange_kernel(loads, elems, places, codes, g, r, table, m, t, held, packed, ed, es, er, ee, eo, ms, mz, mr, mzr, own, hsem, *sems):
+def exchange_kernel(loads, elems, places, codes, row_of, col_idx, vals, g, r, table, part, m, v, t, held, packed, ed, es, er, ee, eo, ms, mz, mr, mzr, own, hsem, vsem, *sems):
     place = Place()
     r = r.reshape(4, 16, PAIR, LANES)
     gather = Gather(place, g.reshape(32 * ROWS, 2 * LANES), 0, sems)
@@ -252,6 +253,13 @@
     mine.start()
     holding = pltpu.make_async_copy(elems, held, hsem)
     holding.start()
+
+    def fetch(j, _):
+        first = (2 * j + place.core) * CHUNK
+        pltpu.make_async_copy(vals.at[pl.ds(first, CHUNK)], v.at[pl.ds(j * CHUNK, CHUNK)], vsem).start()
+        return 0
+
+    lax.fori_loop(0, v.shape[0] // CHUNK, fetch, 0)
 
     mine.wait()
     pl.semaphore_wait(barrier, 6 + 3 + 15)
@@ -324,7 +332,20 @@
     wait_bytes(m.at[level], mr)
     for dz in (1, 2, 3):
         send(m.at[level], m.at[level], mz, mzr, place.above(dz))
+    part[...] = jnp.zeros_like(part)
+    wait_bytes(v, vsem)
     gather.finish()
+    for first, last, rows in STORED_ROWS:
+
+        def stored(j):
+            for u in range(CHUNK):
+                s = (2 * j + place.core) * CHUNK + u
+                product = jnp.dot(v[j * CHUNK + u], g[col_idx[s]], preferred_element_type=jnp.float32)
+                row = row_of[s]
+                for i in rows:
+                    part[i] += jnp.where(row == i + 1, product, 0.0)
+
+        loop(first, last, stored)
     wait_bytes(r.at[pl.ds(0, 3)], er)
     wait_bytes(m.at[pl.ds(0, 3)], mzr)
     wait_bytes(r.at[pl.ds(0, 3)], es)
@@ -334,7 +355,7 @@
     table[...] = m[:, :, 0, :].reshape(64, LANES)
 
 
-def exchange(loads, elems, places, codes):
+def exchange(loads, elems, places, codes, row_of, col_idx, vals):
     hbm = pl.BlockSpec(memory_space=pltpu.HBM)
     vmem = pl.BlockSpec(memory_space=pltpu.VMEM)
     dma = pltpu.SemaphoreType.DMA
@@ -344,16 +365,21 @@
             pltpu.VMEM((128, BS, 2 * LANES), jnp.bfloat16),
             pltpu.VMEM((64, PAIR, LANES), jnp.bfloat16),
             pltpu.VMEM((64, LANES), jnp.int32),
+            pltpu.VMEM((4, BS, 2 * LANES), jnp.float32),
         ],
         in_specs=[
             hbm,
             hbm,
             pl.BlockSpec(memory_space=pltpu.SMEM),
             hbm,
+            pl.BlockSpec(memory_space=pltpu.SMEM),
+            pl.BlockSpec(memory_space=pltpu.SMEM),
+            hbm,
         ],
-        out_specs=[vmem, vmem, vmem],
+        out_specs=[vmem] * 4,
         scratch_shapes=[
             pltpu.VMEM((4, 16, 8, LANES), jnp.int32),
+            pltpu.VMEM((vals.shape[0] // 2, BS, BS), jnp.bfloat16),
             pltpu.VMEM((16, PAIR, LANES), jnp.bfloat16),
             pltpu.VMEM(elems.shape, jnp.bfloat16),
             pltpu.VMEM((16, 2, PAIR, LANES), jnp.bfloat16),
@@ -362,6 +388,7 @@
             dma,
             dma((16,)),
             dma((16,)),
+            dma,
             dma,
             dma,
             dma,
@@ -372,7 +399,7 @@
         ],
         compiler_params=pltpu.CompilerParams(collective_id=1, has_side_effects=True, vmem_limit_bytes=30 << 20),
         name="exchange",
-    )(loads, elems, places, codes)
+    )(loads, elems, places, codes, row_of, col_idx, vals)
 
 
 def share_sum(place, part, came, send_sem, recv_sem):
@@ -464,24 +491,10 @@
     )(part)
 
 
-def product_kernel(row_of, col_idx, table, vals, pairs, panel, out, vbuf, acc, code, sem, vsem):
-    fetch = pltpu.make_async_copy(table, code, sem)
-    fetch.start()
-    core = lax.rem(lax.axis_index("rep"), 2)
-    blk = lax.axis_index("blk")
-    v_count = vals.shape[0] // (2 * CHUNK)
-
-    def v_copy(j, slot):
-        first = (2 * j + core) * CHUNK
-        return pltpu.make_async_copy(vals.at[pl.ds(first, CHUNK)], vbuf.at[slot], vsem.at[slot])
-
-    for j in range(DEPTH):
-        v_copy(j, j).start()
-    acc[...] = jnp.zeros_like(acc)
+def add_pairs(code, blk, pairs, panel, acc):
     none = jnp.zeros((64, 2 * LANES), jnp.bfloat16)
-    fetch.wait()
-
-    def e_step(j, _):
+
+    def step(j, _):
         for u in range(2 * CHUNK):
             at = j * CHUNK + u // 2
             held = code[at, blk * 2 + u % 2]
@@ -494,7 +507,34 @@
             )
         return 0
 
-    lax.fori_loop(0, pairs.shape[0] // CHUNK, e_step, 0)
+    lax.fori_loop(0, pairs.shape[0] // CHUNK, step, 0)
+
+
+def pair_kernel(start, table, pairs, panel, out, acc, code, sem):
+    fetch = pltpu.make_async_copy(table, code, sem)
+    fetch.start()
+    acc[0] = jnp.zeros_like(acc[0])
+    acc[1:] = start[...]
+    fetch.wait()
+    add_pairs(code, lax.axis_index("blk"), pairs, panel, acc)
+    out[...] = acc[1:].reshape(out.shape)
+
+
+def product_kernel(row_of, col_idx, table, vals, pairs, panel, out, vbuf, acc, code, sem, vsem):
+    fetch = pltpu.make_async_copy(table, code, sem)
+    fetch.start()
+    core = lax.rem(lax.axis_index("rep"), 2)
+    v_count = vals.shape[0] // (2 * CHUNK)
+
+    def v_copy(j, slot):
+        first = (2 * j + core) * CHUNK
+        return pltpu.make_async_copy(vals.at[pl.ds(first, CHUNK)], vbuf.at[slot], vsem.at[slot])
+
+    for j in range(DEPTH):
+        v_copy(j, j).start()
+    acc[...] = jnp.zeros_like(acc)
+    fetch.wait()
+    add_pairs(code, lax.axis_index("blk"), pairs, panel, acc)
 
     def v_step(j, _):
         slot = lax.rem(j, DEPTH)
@@ -513,25 +553,39 @@
     out[...] = acc[1:].reshape(out.shape)
 
 
-def products(row_of, col_idx, table, vals, elems, g):
+def products(row_of, col_idx, table, vals, pairs, g, start=None):
     smem = pl.BlockSpec(memory_space=pltpu.SMEM)
     vmem = pl.BlockSpec(memory_space=pltpu.VMEM)
     hbm = pl.BlockSpec(memory_space=pltpu.HBM)
+    work = [
+        pltpu.VMEM((5, BS, 2 * LANES), jnp.float32),
+        pltpu.SMEM((64, LANES), jnp.int32),
+        pltpu.SemaphoreType.DMA,
+    ]
+    out = pltpu.VMEM((ROWS, 2 * LANES), jnp.float32)
+    if start is not None:
+        return pl.pallas_call(
+            pair_kernel,
+            out_shape=out,
+            in_specs=[vmem] * 4,
+            out_specs=vmem,
+            scratch_shapes=work,
+            compiler_params=pltpu.CompilerParams(vmem_limit_bytes=4 << 20),
+            name="pairs",
+        )(start, table, pairs, g)
     return pl.pallas_call(
         product_kernel,
-        out_shape=pltpu.VMEM((ROWS, 2 * LANES), jnp.float32),
+        out_shape=out,
         in_specs=[smem, smem, vmem, hbm, vmem, vmem],
         out_specs=vmem,
         scratch_shapes=[
             pltpu.VMEM((DEPTH, CHUNK, BS, BS), jnp.bfloat16),
-            pltpu.VMEM((5, BS, 2 * LANES), jnp.float32),
-            pltpu.SMEM((64, LANES), jnp.int32),
-            pltpu.SemaphoreType.DMA,
+            *work,
             pltpu.SemaphoreType.DMA((DEPTH,)),
         ],
         compiler_params=pltpu.CompilerParams(vmem_limit_bytes=12 << 20),
         name="products",
-    )(row_of, col_idx, table, vals, elems, g)
+    )(row_of, col_idx, table, vals, pairs, g)
 
 
 def body(loads, values, row_ptr, col_idx, elem_vals, elem_owner, elem_row, elem_col):
@@ -548,10 +602,10 @@
     positions = jnp.arange(values.shape[0], dtype=jnp.int32)
     row = 1 + jnp.sum((positions[:, None] >= row_ptr[0, 1:][None, :]).astype(jnp.int32), axis=1)
     row_of = jnp.where(row > 4, 0, row)
-    g, r, table = exchange(loads, elem_vals, places, codes)
+    g, r, table, part = exchange(loads, elem_vals, places, codes, row_of, col_idx, values)
 
     apply = functools.partial(products, row_of, col_idx, table, values, r)
-    part = apply(g)
+    part = apply(g, start=part)
     g2 = gather_first(part)
     return sum_cores(apply(g2))
 

time: 191 us -> 184 us (0.963)
  Pallas kernels: 185 us -> 177 us
    pallas_call x2, Pallas kernels: 24.9 us -> 17.7 us  [the longest x1 12.4 us: products(): pl.pallas_call(product_kernel, out_shape=out, in_specs=[smem, smem, vmem,...]
where the time goes in v1:
time: 184 us; the launch traced here: 182 us
  Pallas kernels  177 us (96%)
  local copies, waits for them, and re-layouts  3.09 us (2%)
    pallas_call x1, Pallas kernels, exchange(): pl.pallas_call(exchange_kernel, out_shape=[pltpu.VMEM((128, BS, 2 * LANES...  121 us
    pallas_call x1, Pallas kernels, gather_first(): pl.pallas_call(gather_kernel, out_shape=pltpu.VMEM((128, BS, 2 * LANES),...  37.3 us
    pallas_call x1, Pallas kernels, products(): pl.pallas_call(product_kernel, out_shape=out, in_specs=[smem, smem, vmem,...  12.4 us
    pallas_call x1, Pallas kernels, products(): pl.pallas_call(pair_kernel, out_shape=out, in_specs=[vmem] * 4, out_specs...  5.32 us

profile of v1, /device:TPU:0, one launch (start us, length us, event | category | flops | bytes accessed | tf_op | source)
XLA Modules:
  0.0 182.4 jit_solution(4753669740750778449)
XLA Ops:
  0.0 0.7 slice_bitcast_fusion
  0.7 0.9 convert_reduce_fusion
  1.6 0.7 multiply_add_fusion
  2.3 0.1 select_reduce_fusion
  2.4 0.1 convert_reduce_fusion.1
  2.5 0.0 copy-start
  2.5 0.9 copy-done
  3.5 0.0 copy-start.1
  3.5 0.7 copy-done.1
  4.1 120.5 %exchange.1 = (bf16[128,192,256]{2,1,0:T(8,128)(2,1)S(1)}, bf16[64,576,128]{2,1,0:T(8,128)(2,1)S(1)}, s32[64,128]{1,0:T(8,128)S(1)}, f32[4,192,256]{2,1,0:T(8,128)S(1)}) custom-call(bf16[768,128]{1,0:T(8,128)(2,1)S(1)} %copy-done, bf16[32,192,192]{2,1,0:T(8,128)(2,1)} %elems.1, s32[128]{0:T(128)S(1)} %get-tuple-element.14.places, ...), custom_call_target="tpu_custom_call" | custom-call | tf_op jit(solution)/shard_map/exchange/pallas_call | solution.py:362
  124.7 5.3 %pairs.1.part = f32[768,256]{1,0:T(8,128)S(1)} custom-call(f32[4,192,256]{2,1,0:T(8,128)S(1)} %get-tuple-element.11.start, s32[64,128]{1,0:T(8,128)S(1)} %get-tuple-element.9.table, bf16[64,576,128]{2,1,0:T(8,128)(2,1)S(1)} %get-tuple-element.10.pairs, bf16[128,192,256]{2,1,0:T(8,128)(2,1)S(1)} %get-tuple-element.12.panel), custom_call_target="tpu_custom_call" | custom-call | tf_op jit(solution)/shard_map/pairs/pallas_call | solution.py:567
  130.0 0.0 copy-start.2
  130.0 37.3 %gather_first.1.panel = bf16[128,192,256]{2,1,0:T(8,128)(2,1)S(1)} custom-call(f32[768,256]{1,0:T(8,128)S(1)} %pairs.1.part), custom_call_target="tpu_custom_call" | custom-call | tf_op jit(solution)/shard_map/gather_first/pallas_call | solution.py:458
  167.3 0.0 copy-done.2
  167.3 12.4 %products.1.part = f32[768,256]{1,0:T(8,128)S(1)} custom-call(s32[288]{0:T(512)S(1)} %compare_select_fusion.row_of, s32[288]{0:T(512)S(1)} %copy-done.2, s32[64,128]{1,0:T(8,128)S(1)} %get-tuple-element.9.table, bf16[288,192,192]{2,1,0:T(8,128)(2,1)} %vals.3, bf16[64,576,128]{2,1,0:T(8,128)(2,1)S(1)} %get-tuple-element.10.pairs, ...), custom_call_target="tpu_custom_call" | custom-call | tf_op jit(solution)/shard_map/products/pallas_call | solution.py:576
  179.8 1.9 %sum_cores.1 = f32[768,128]{1,0:T(8,128)S(1)} custom-call(f32[768,256]{1,0:T(8,128)S(1)} %products.1.part), custom_call_target="tpu_custom_call" | custom-call | tf_op jit(solution)/shard_map/sum_cores/pallas_call | solution.py:483
  181.7 0.7 copy.10
  (2 shorter events, 0.0 us)
Async XLA Ops:
  2.5 0.9 copy-start
  3.5 0.7 copy-start.1
  130.0 37.3 %copy-start.2 = (s32[288]{0:T(512)S(1)}, s32[288]{0:T(512)}, u32[]{:S(2)}) copy-start(s32[288]{0:T(512)} %col_idx.3) | copy-start | bytes 3460

commit v2 on v1

--- a/solution.py
+++ b/solution.py
@@ -235,11 +235,12 @@
     return barrier
 
 
-def exchange_kernel(loads, elems, places, codes, row_of, col_idx, vals, g, r, table, part, m, v, t, held, packed, ed, es, er, ee, eo, ms, mz, mr, mzr, own, hsem, vsem, *sems):
+def exchange_kernel(loads, elems, places, codes, row_of, col_idx, vals, g, r, table, part, m, near, v, t, held, packed, ed, es, er, ee, eo, ms, mz, mr, mzr, own, hsem, vsem, nsem, *sems):
     place = Place()
     r = r.reshape(4, 16, PAIR, LANES)
     gather = Gather(place, g.reshape(32 * ROWS, 2 * LANES), 0, sems)
     spot = place.y * 4 + place.x
+    me = place.block(0, 0, 0)
     level = place.zh * 2 + place.zl
     barrier = greet(gather.peers() + [place.above(dz) for dz in (1, 2, 3)])
 
@@ -346,6 +347,19 @@
                     part[i] += jnp.where(row == i + 1, product, 0.0)
 
         loop(first, last, stored)
+    here = pl.ds(pl.multiple_of(level * 16, 16), 16)
+    table[here, :] = m[level, :, 0, :]
+    pltpu.make_async_copy(table.at[here], near, nsem).start()
+    wait_bytes(near, nsem)
+
+    def arrived(j):
+        for u in range(CHUNK):
+            at = j * (CHUNK // 2) + u // 2
+            row, product = pair_product(near, at, me, u % 2, r.at[level, at], g)
+            for i in range(4):
+                part[i] += jnp.where(row == i + 1, product, 0.0)
+
+    loop(0, 2, arrived)
     wait_bytes(r.at[pl.ds(0, 3)], er)
     wait_bytes(m.at[pl.ds(0, 3)], mzr)
     wait_bytes(r.at[pl.ds(0, 3)], es)
@@ -379,6 +393,7 @@
         out_specs=[vmem] * 4,
         scratch_shapes=[
             pltpu.VMEM((4, 16, 8, LANES), jnp.int32),
+            pltpu.SMEM((16, LANES), jnp.int32),
             pltpu.VMEM((vals.shape[0] // 2, BS, BS), jnp.bfloat16),
             pltpu.VMEM((16, PAIR, LANES), jnp.bfloat16),
             pltpu.VMEM(elems.shape, jnp.bfloat16),
@@ -388,6 +403,7 @@
             dma,
             dma((16,)),
             dma((16,)),
+            dma,
             dma,
             dma,
             dma,
@@ -491,23 +507,28 @@
     )(part)
 
 
-def add_pairs(code, blk, pairs, panel, acc):
+def pair_product(code, at, blk, k, pair, panel):
+    held = code[at, blk * 2 + k]
     none = jnp.zeros((64, 2 * LANES), jnp.bfloat16)
+    x = panel[held & 127]
+    ends = [x[LANES:], none] if k == 0 else [none, x[LANES:]]
+    block = jnp.concatenate([pair[pl.ds(k * BS, BS)], pair[pl.ds(2 * BS, BS)]], axis=1)
+    product = jnp.dot(block, jnp.concatenate([x[:LANES], *ends], axis=0), preferred_element_type=jnp.float32)
+    return lax.shift_right_logical(held, 7), product
+
+
+def add_pairs(code, first, count, pairs, panel, acc):
+    blk = lax.axis_index("blk")
 
     def step(j, _):
+        plane = lax.rem(first + j, 4)
         for u in range(2 * CHUNK):
-            at = j * CHUNK + u // 2
-            held = code[at, blk * 2 + u % 2]
-            row = lax.shift_right_logical(held, 7)
-            x = panel[held & 127]
-            ends = [x[LANES:], none] if u % 2 == 0 else [none, x[LANES:]]
-            block = jnp.concatenate([pairs[at, pl.ds(u % 2 * BS, BS)], pairs[at, pl.ds(2 * BS, BS)]], axis=1)
-            acc[row] += jnp.dot(
-                block, jnp.concatenate([x[:LANES], *ends], axis=0), preferred_element_type=jnp.float32
-            )
+            at = plane * CHUNK + u // 2
+            row, product = pair_product(code, at, blk, u % 2, pairs.at[at], panel)
+            acc[row] += product
         return 0
 
-    lax.fori_loop(0, pairs.shape[0] // CHUNK, step, 0)
+    lax.fori_loop(0, count, step, 0)
 
 
 def pair_kernel(start, table, pairs, panel, out, acc, code, sem):
@@ -516,7 +537,8 @@
     acc[0] = jnp.zeros_like(acc[0])
     acc[1:] = start[...]
     fetch.wait()
-    add_pairs(code, lax.axis_index("blk"), pairs, panel, acc)
+    place = Place()
+    add_pairs(code, place.zh * 2 + place.zl + 1, 3, pairs, panel, acc)
     out[...] = acc[1:].reshape(out.shape)
 
 
@@ -534,7 +556,7 @@
         v_copy(j, j).start()
     acc[...] = jnp.zeros_like(acc)
     fetch.wait()
-    add_pairs(code, lax.axis_index("blk"), pairs, panel, acc)
+    add_pairs(code, 0, 4, pairs, panel, acc)
 
     def v_step(j, _):
         slot = lax.rem(j, DEPTH)

time: 184 us -> 183 us (level)
  no operation moved by 1% of the time
where the time goes in v2:
time: 183 us; the launch traced here: 181 us
  Pallas kernels  176 us (96%)
  local copies, waits for them, and re-layouts  3.09 us (2%)
    pallas_call x1, Pallas kernels, exchange(): pl.pallas_call(exchange_kernel, out_shape=[pltpu.VMEM((128, BS, 2 * LANES...  121 us
    pallas_call x1, Pallas kernels, gather_first(): pl.pallas_call(gather_kernel, out_shape=pltpu.VMEM((128, BS, 2 * LANES),...  37.3 us
    pallas_call x1, Pallas kernels, products(): pl.pallas_call(product_kernel, out_shape=out, in_specs=[smem, smem, vmem,...  12.3 us
    pallas_call x1, Pallas kernels, products(): pl.pallas_call(pair_kernel, out_shape=out, in_specs=[vmem] * 4, out_specs...  4.3 us

profile of v2, /device:TPU:0, one launch (start us, length us, event | category | flops | bytes accessed | tf_op | source)
XLA Modules:
  0.0 181.3 jit_solution(17966999188119980320)
XLA Ops:
  0.0 0.7 slice_bitcast_fusion
  0.7 0.9 convert_reduce_fusion
  1.6 0.7 multiply_add_fusion
  2.3 0.1 select_reduce_fusion
  2.4 0.1 convert_reduce_fusion.1
  2.5 0.0 copy-start
  2.5 0.9 copy-done
  3.5 0.0 copy-start.1
  3.5 0.7 copy-done.1
  4.1 120.5 %exchange.1 = (bf16[128,192,256]{2,1,0:T(8,128)(2,1)S(1)}, bf16[64,576,128]{2,1,0:T(8,128)(2,1)S(1)}, s32[64,128]{1,0:T(8,128)S(1)}, f32[4,192,256]{2,1,0:T(8,128)S(1)}) custom-call(bf16[768,128]{1,0:T(8,128)(2,1)S(1)} %copy-done, bf16[32,192,192]{2,1,0:T(8,128)(2,1)} %elems.1, s32[128]{0:T(128)S(1)} %get-tuple-element.14.places, ...), custom_call_target="tpu_custom_call" | custom-call | tf_op jit(solution)/shard_map/exchange/pallas_call | solution.py:376
  124.7 4.3 %pairs.1.part = f32[768,256]{1,0:T(8,128)S(1)} custom-call(f32[4,192,256]{2,1,0:T(8,128)S(1)} %get-tuple-element.11.start, s32[64,128]{1,0:T(8,128)S(1)} %get-tuple-element.9.table, bf16[64,576,128]{2,1,0:T(8,128)(2,1)S(1)} %get-tuple-element.10.pairs, bf16[128,192,256]{2,1,0:T(8,128)(2,1)S(1)} %get-tuple-element.12.panel), custom_call_target="tpu_custom_call" | custom-call | tf_op jit(solution)/shard_map/pairs/pallas_call | solution.py:589
  129.0 0.0 copy-start.2
  129.0 37.3 %gather_first.1.panel = bf16[128,192,256]{2,1,0:T(8,128)(2,1)S(1)} custom-call(f32[768,256]{1,0:T(8,128)S(1)} %pairs.1.part), custom_call_target="tpu_custom_call" | custom-call | tf_op jit(solution)/shard_map/gather_first/pallas_call | solution.py:474
  166.3 0.0 copy-done.2
  166.3 12.3 %products.1.part = f32[768,256]{1,0:T(8,128)S(1)} custom-call(s32[288]{0:T(512)S(1)} %compare_select_fusion.row_of, s32[288]{0:T(512)S(1)} %copy-done.2, s32[64,128]{1,0:T(8,128)S(1)} %get-tuple-element.9.table, bf16[288,192,192]{2,1,0:T(8,128)(2,1)} %vals.3, bf16[64,576,128]{2,1,0:T(8,128)(2,1)S(1)} %get-tuple-element.10.pairs, ...), custom_call_target="tpu_custom_call" | custom-call | tf_op jit(solution)/shard_map/products/pallas_call | solution.py:598
  178.7 1.9 %sum_cores.1 = f32[768,128]{1,0:T(8,128)S(1)} custom-call(f32[768,256]{1,0:T(8,128)S(1)} %products.1.part), custom_call_target="tpu_custom_call" | custom-call | tf_op jit(solution)/shard_map/sum_cores/pallas_call | solution.py:499
  180.6 0.7 copy.10
  (2 shorter events, 0.0 us)
Async XLA Ops:
  2.5 0.9 copy-start
  3.5 0.7 copy-start.1
  129.0 37.3 %copy-start.2 = (s32[288]{0:T(512)S(1)}, s32[288]{0:T(512)}, u32[]{:S(2)}) copy-start(s32[288]{0:T(512)} %col_idx.3) | copy-start | bytes 3460

commit v3 on v2

--- a/solution.py
+++ b/solution.py
@@ -14,7 +14,8 @@
 HALF = ROWS // 2
 PAIR = 3 * BS
 CHUNK = 16
-DEPTH = 4
+DEPTH = 6
+GROUP = 3
 STORED_ROWS = ((0, 1, (0,)), (1, 2, (0, 1)), (2, 3, (0, 1, 2)), (3, 5, (1, 2, 3)), (5, 7, (2, 3)), (7, 9, (3,)))
 
 
@@ -558,20 +559,25 @@
     fetch.wait()
     add_pairs(code, 0, 4, pairs, panel, acc)
 
-    def v_step(j, _):
-        slot = lax.rem(j, DEPTH)
-        v_copy(j, slot).wait()
-        for u in range(CHUNK):
-            s = (2 * j + core) * CHUNK + u
-            acc[row_of[s]] += jnp.dot(vbuf[slot, u], panel[col_idx[s]], preferred_element_type=jnp.float32)
-
-        @pl.when(j + DEPTH < v_count)
+    def v_step(group, _):
+        for i in range(GROUP):
+            v_copy(group * GROUP + i, lax.rem(group * GROUP + i, DEPTH)).wait()
+        for i in range(GROUP):
+            j = group * GROUP + i
+            slot = lax.rem(j, DEPTH)
+            for u in range(CHUNK):
+                s = (2 * j + core) * CHUNK + u
+                acc[row_of[s]] += jnp.dot(vbuf[slot, u], panel[col_idx[s]], preferred_element_type=jnp.float32)
+
+        @pl.when((group + 1) * GROUP + DEPTH - GROUP < v_count)
         def _():
-            v_copy(j + DEPTH, slot).start()
+            for i in range(GROUP):
+                j = group * GROUP + i
+                v_copy(j + DEPTH, lax.rem(j, DEPTH)).start()
 
         return 0
 
-    lax.fori_loop(0, v_count, v_step, 0)
+    lax.fori_loop(0, v_count // GROUP, v_step, 0)
     out[...] = acc[1:].reshape(out.shape)
 
 
@@ -605,7 +611,7 @@
             *work,
             pltpu.SemaphoreType.DMA((DEPTH,)),
         ],
-        compiler_params=pltpu.CompilerParams(vmem_limit_bytes=12 << 20),
+        compiler_params=pltpu.CompilerParams(vmem_limit_bytes=14 << 20),
         name="products",
     )(row_of, col_idx, table, vals, pairs, g)
 

time: 183 us -> 183 us (level)
  no operation moved by 1% of the time
where the time goes in v3:
time: 183 us; the launch traced here: 181 us
  Pallas kernels  176 us (96%)
  local copies, waits for them, and re-layouts  3.09 us (2%)
    pallas_call x1, Pallas kernels, exchange(): pl.pallas_call(exchange_kernel, out_shape=[pltpu.VMEM((128, BS, 2 * LANES...  121 us
    pallas_call x1, Pallas kernels, gather_first(): pl.pallas_call(gather_kernel, out_shape=pltpu.VMEM((128, BS, 2 * LANES),...  37.3 us
    pallas_call x1, Pallas kernels, products(): pl.pallas_call(product_kernel, out_shape=out, in_specs=[smem, smem, vmem,...  12.1 us
    pallas_call x1, Pallas kernels, products(): pl.pallas_call(pair_kernel, out_shape=out, in_specs=[vmem] * 4, out_specs...  4.3 us

profile of v3, /device:TPU:0, one launch (start us, length us, event | category | flops | bytes accessed | tf_op | source)
XLA Modules:
  0.0 181.1 jit_solution(2497085291820741713)
XLA Ops:
  0.0 0.7 slice_bitcast_fusion
  0.7 0.9 convert_reduce_fusion
  1.6 0.7 multiply_add_fusion
  2.3 0.1 select_reduce_fusion
  2.4 0.1 convert_reduce_fusion.1
  2.5 0.0 copy-start
  2.5 0.9 copy-done
  3.5 0.0 copy-start.1
  3.5 0.7 copy-done.1
  4.1 120.5 %exchange.1 = (bf16[128,192,256]{2,1,0:T(8,128)(2,1)S(1)}, bf16[64,576,128]{2,1,0:T(8,128)(2,1)S(1)}, s32[64,128]{1,0:T(8,128)S(1)}, f32[4,192,256]{2,1,0:T(8,128)S(1)}) custom-call(bf16[768,128]{1,0:T(8,128)(2,1)S(1)} %copy-done, bf16[32,192,192]{2,1,0:T(8,128)(2,1)} %elems.1, s32[128]{0:T(128)S(1)} %get-tuple-element.14.places, ...), custom_call_target="tpu_custom_call" | custom-call | tf_op jit(solution)/shard_map/exchange/pallas_call | solution.py:377
  124.7 4.3 %pairs.1.part = f32[768,256]{1,0:T(8,128)S(1)} custom-call(f32[4,192,256]{2,1,0:T(8,128)S(1)} %get-tuple-element.11.start, s32[64,128]{1,0:T(8,128)S(1)} %get-tuple-element.9.table, bf16[64,576,128]{2,1,0:T(8,128)(2,1)S(1)} %get-tuple-element.10.pairs, bf16[128,192,256]{2,1,0:T(8,128)(2,1)S(1)} %get-tuple-element.12.panel), custom_call_target="tpu_custom_call" | custom-call | tf_op jit(solution)/shard_map/pairs/pallas_call | solution.py:595
  129.0 0.0 copy-start.2
  129.0 37.3 %gather_first.1.panel = bf16[128,192,256]{2,1,0:T(8,128)(2,1)S(1)} custom-call(f32[768,256]{1,0:T(8,128)S(1)} %pairs.1.part), custom_call_target="tpu_custom_call" | custom-call | tf_op jit(solution)/shard_map/gather_first/pallas_call | solution.py:475
  166.3 0.0 copy-done.2
  166.3 12.1 %products.1.part = f32[768,256]{1,0:T(8,128)S(1)} custom-call(s32[288]{0:T(512)S(1)} %compare_select_fusion.row_of, s32[288]{0:T(512)S(1)} %copy-done.2, s32[64,128]{1,0:T(8,128)S(1)} %get-tuple-element.9.table, bf16[288,192,192]{2,1,0:T(8,128)(2,1)} %vals.3, bf16[64,576,128]{2,1,0:T(8,128)(2,1)S(1)} %get-tuple-element.10.pairs, ...), custom_call_target="tpu_custom_call" | custom-call | tf_op jit(solution)/shard_map/products/pallas_call | solution.py:604
  178.4 1.9 %sum_cores.1 = f32[768,128]{1,0:T(8,128)S(1)} custom-call(f32[768,256]{1,0:T(8,128)S(1)} %products.1.part), custom_call_target="tpu_custom_call" | custom-call | tf_op jit(solution)/shard_map/sum_cores/pallas_call | solution.py:500
  180.3 0.7 copy.10
  (2 shorter events, 0.0 us)
Async XLA Ops:
  2.5 0.9 copy-start
  3.5 0.7 copy-start.1
  129.0 37.3 %copy-start.2 = (s32[288]{0:T(512)S(1)}, s32[288]{0:T(512)}, u32[]{:S(2)}) copy-start(s32[288]{0:T(512)} %col_idx.3) | copy-start | bytes 3460
